TPU v7x, 256 devices: a whole 4x4x8 slice. The times are simulated.
256 devices in a mesh: dp: 32 (over z_hi, x, core), tensor: 8 (over z_lo, y).
Axes of the slice: x: 4, y: 4, z: 8 (z_hi: 4, z_lo: 2; z = z_hi * 2 + z_lo), core: 2. Of those that a mesh axis runs over, the one named last changes fastest.
Arguments:
- tokens: bfloat16 [4096, 4096], P('dp', 'tensor'), may hold values from -6 to 6
- gate_pre: bfloat16 [4096, 14336], P('dp', 'tensor'), may hold values from -12 to 12
- up_act: bfloat16 [4096, 14336], P('dp', 'tensor'), may hold values from -6 to 6
- hidden_cot: bfloat16 [4096, 14336], P('dp', 'tensor'), may hold values from -6 to 6
- source_ids: int32 [4096], P('dp'), may hold values from 0 to 63
- data_weight: float32 [64], replicated, may hold values from 0.25 to 4
- grad: float32 [4096, 14336], P('dp', 'tensor'), may hold values from -6 to 6
- moment_m: float32 [4096, 14336], P('dp', 'tensor'), may hold values from -0.0006 to 0.0006
- moment_v: float32 [4096, 14336], P('dp', 'tensor'), may hold values from 1e-09 to 1e-07
- val_adjoint: float32 [4096, 14336], P('dp', 'tensor'), may hold values from -17000 to 17000
Outputs:
- curvature: float32 [4096, 14336], P('dp', 'tensor')
- source_grad: float32 [64], replicated
All inputs are finite; a program needn't handle non-finite values.
Results may differ from a plain program's by a relative error of at most 0.029.
Values may be sent and summed in bfloat16 or wider, within the bound.
A program may use at most 128 MiB of HBM per device.

v0:
```python
import jax
import jax.numpy as jnp
from jax import lax
from jax.sharding import PartitionSpec as P

CLIP_NORM = 1.0
LEARN_RATE = 0.00015
BETA_ONE = 0.9
BETA_TWO = 0.95
ADAM_EPSILON = 1e-08
NORM_EPSILON = 1e-06


def clip_terms(total_sq):
    scaled = CLIP_NORM * lax.rsqrt(total_sq)
    return jnp.minimum(scaled, 1.0)


def pulled_back(grad, moment_m, moment_v, val_adjoint, clip_factor):
    clipped = clip_factor * grad
    moment_new = BETA_ONE * moment_m + (1.0 - BETA_ONE) * clipped
    second_new = BETA_TWO * moment_v + (1.0 - BETA_TWO) * clipped * clipped
    root_v = jnp.sqrt(second_new)
    denominator = root_v + ADAM_EPSILON
    jacobian = -LEARN_RATE * (
        (1.0 - BETA_ONE) / denominator
        - moment_new * (1.0 - BETA_TWO) * clipped / (denominator * denominator * root_v)
    )
    return jacobian * val_adjoint


def activation_terms(gate_pre, up_act, hidden_cot):
    pre_act = gate_pre.astype(jnp.float32)
    sigma = jax.nn.sigmoid(pre_act)
    first_slope = sigma * (1.0 + pre_act * (1.0 - sigma))
    second_slope = sigma * (1.0 - sigma) * (2.0 + pre_act * (1.0 - 2.0 * sigma))
    coupling = up_act.astype(jnp.float32) * hidden_cot.astype(jnp.float32)
    return (coupling * first_slope, coupling * second_slope)


def body(
    tokens,
    gate_pre,
    up_act,
    hidden_cot,
    source_ids,
    data_weight,
    grad,
    moment_m,
    moment_v,
    val_adjoint,
):
    total_sq = lax.psum(jnp.sum(grad * grad), ("dp", "tensor")) + NORM_EPSILON
    clip_factor = clip_terms(total_sq)
    pulled = pulled_back(grad, moment_m, moment_v, val_adjoint, clip_factor)
    tangent = (clip_factor * pulled).astype(jnp.bfloat16)
    whole_rows = lax.all_gather(tokens, "tensor", axis=1, tiled=True)
    block_size = tokens.shape[0]
    total_tokens = block_size * lax.axis_size("dp")
    token_cols = whole_rows
    projected = jnp.dot(
        token_cols,
        lax.all_gather(tangent, "dp", axis=0, tiled=True),
        preferred_element_type=jnp.float32,
    )
    first_order, second_order = activation_terms(gate_pre, up_act, hidden_cot)
    source_index = jnp.arange(data_weight.shape[0], dtype=jnp.int32)
    onehot = (source_ids[:, None] == source_index[None, :]).astype(jnp.float32)
    weight_tok = jnp.sum(onehot * data_weight[None, :], axis=1) / total_tokens
    mixed = (weight_tok[:, None] * second_order * projected).astype(jnp.bfloat16)
    token_cols = whole_rows
    curvature = lax.psum_scatter(
        lax.dot_general(
            token_cols, mixed, (((0,), (0,)), ((), ())), preferred_element_type=jnp.float32
        ).astype(jnp.bfloat16),
        "dp",
        scatter_dimension=0,
        tiled=True,
    ).astype(jnp.float32)
    per_tok = jnp.sum(projected * first_order, axis=1)
    per_tok = lax.psum(per_tok, "tensor")
    local_sums = jnp.sum(onehot * per_tok[:, None], axis=0)
    source_grad = lax.psum(local_sums, "dp") / total_tokens
    return (curvature, source_grad)


def solution(mesh):
    in_specs = (
        P("dp", "tensor"),
        P("dp", "tensor"),
        P("dp", "tensor"),
        P("dp", "tensor"),
        P("dp"),
        P(),
        P("dp", "tensor"),
        P("dp", "tensor"),
        P("dp", "tensor"),
        P("dp", "tensor"),
    )
    out_specs = (P("dp", "tensor"), P())
    return jax.shard_map(body, mesh=mesh, in_specs=in_specs, out_specs=out_specs, check_vma=False)
```

profile of v0, /device:TPU:1, one launch (start us, length us, event | category | flops | bytes accessed | tf_op | source)
XLA Modules:
  0.0 409.2 jit_solution(17372992204316408948)
XLA Ops:
  7.2 0.0 all-gather.5.cloned.1.call-start
  7.2 0.7 all-gather.5.cloned.1.call-update
  7.9 0.0 all-gather.3.cloned.1.call-start
  7.9 2.0 multiply_reduce_fusion
  10.0 81.7 %psum.21 = f32[]{:T(128)} all-reduce(f32[]{:T(128)} %multiply_reduce_fusion), channel_id=1, replica_groups=mesh['dp'=32,'tensor'=8] {'dp','tensor'}, use_global_device_ids=true, to_apply=%region_2.0 | all-reduce | flops 1 | bytes 8 | tf_op jit(solution)/shard_map/psum | solution.py:53
  92.4 3.6 multiply_convert_fusion
  96.0 0.0 all-gather.3.cloned.1.call-update
  96.1 0.0 reduce-scatter.4.cloned.1.call-start
  96.1 1.3 copy.22
  97.4 1.3 copy.20
  98.7 1.3 copy.21
  100.0 0.0 all-gather.5.cloned.1.call-done
  100.0 89.2 %all-gather.3.cloned.1.call-done = bf16[4096,1792]{1,0:T(8,128)(2,1)} async-done(((bf16[128,1792]{1,0:T(8,128)(2,1)}), bf16[4096,1792]{1,0:T(8,128)(2,1)}) %all-gather.3.cloned.1.call-update) | async-done | bytes 14680080 | tf_op jit(solution)/shard_map/all_gather | solution.py:63
  189.2 7.6 %fusion.14 = (f32[128]{0:T(128)S(1)}, f32[128,1792]{0,1:T(8,128)S(1)}) fusion(bf16[128,1792]{0,1:T(8,128)(2,1)S(1)} %copy.22, bf16[128,1792]{0,1:T(8,128)(2,1)S(1)} %copy.21, bf16[128,1792]{0,1:T(8,128)(2,1)S(1)} %copy.20, bf16[4096,1792]{1,0:T(8,128)(2,1)} %all-gather.3.cloned.1.call-done, bf16[128,4096]{1,0:T(8,128)(2,1)} %all-gather.5.cloned.1.call-done), kind=kOutput, calls=%fused_computation.21 | convolution fusion | flops 1882259328 | bytes 18022912 | tf_op jit(solution)/shard_map/dot_general | solution.py:61
  196.8 26.8 %psum.22 = f32[128]{0:T(128)S(1)} all-reduce(f32[128]{0:T(128)S(1)} %get-tuple-element.10), channel_id=1, replica_groups=mesh['dp'=32,'tensor'=8] {'tensor'}, use_global_device_ids=true, to_apply=%region_5.0 | all-reduce | flops 128 | bytes 1024 | tf_op jit(solution)/shard_map/psum | solution.py:81
  223.6 0.1 select_reduce_fusion
  223.7 7.4 %fusion = bf16[4096,1792]{0,1:T(8,128)(2,1)} fusion(bf16[128,4096]{1,0:T(8,128)(2,1)S(1)} %copy-done, f32[128,1792]{0,1:T(8,128)S(1)} %get-tuple-element.11, bf16[128,1792]{0,1:T(8,128)(2,1)S(1)} %copy.22, bf16[128,1792]{0,1:T(8,128)(2,1)S(1)} %copy.21, bf16[128,1792]{0,1:T(8,128)(2,1)S(1)} %copy.20, f32[128]{0:T(128)S(1)} %broadcast_multiply_fusion.1), kind=kOutput, calls=%fused_computation.1 | convolution fusion | flops 1890516992 | bytes 18022912 | tf_op jit(solution)/shard_map/dot_general | solution.py:73
  231.1 18.8 %copy.24 = bf16[4096,1792]{1,0:T(8,128)(2,1)} copy(bf16[4096,1792]{0,1:T(8,128)(2,1)} %fusion) | data formatting | bytes 29360128
  249.9 0.0 reduce-scatter.4.cloned.1.call-update
  249.9 73.6 %psum.23 = f32[64]{0:T(128)S(1)} all-reduce(f32[64]{0:T(128)S(1)} %get-tuple-element.8), channel_id=1, replica_groups=mesh['dp'=32,'tensor'=8] {'dp'}, use_global_device_ids=true, to_apply=%region_7.0 | all-reduce | flops 64 | bytes 512 | tf_op jit(solution)/shard_map/psum | solution.py:83
  323.4 0.5 broadcast_multiply_fusion
  324.0 76.3 %reduce-scatter.4.cloned.1.call-done = bf16[128,1792]{1,0:T(8,128)(2,1)} async-done(((bf16[4096,1792]{1,0:T(8,128)(2,1)}), bf16[128,1792]{1,0:T(8,128)(2,1)}) %reduce-scatter.4.cloned.1.call-update) | async-done | bytes 458768
  400.2 1.3 copy.25
  401.5 1.1 copy.23
  (7 shorter events, 0.0 us)
Async XLA Ops:
  7.2 92.8 %all-gather.5.cloned.1.call-start = ((), (), s32[]{:S(2)}) async-start(), calls=%async_computation.2 | async-start | bytes 1179648 | tf_op jit(solution)/shard_map/all_gather | solution.py:57
  7.9 181.3 %all-gather.3.cloned.1.call-start = ((), (), s32[]{:S(2)}) async-start(), calls=%async_computation.1 | async-start | bytes 15138816 | tf_op jit(solution)/shard_map/all_gather | solution.py:63
  96.0 127.5 %copy-start.1 = (s32[128]{0:T(128)S(1)}, s32[128]{0:T(128)}, u32[]{:S(2)}) copy-start(s32[128]{0:T(128)} %param.14) | copy-start | bytes 1540
  96.0 127.5 %copy-start.2 = (f32[64]{0:T(128)S(1)}, f32[64]{0:T(128)}, u32[]{:S(2)}) copy-start(f32[64]{0:T(128)} %param.15) | copy-start | bytes 772
  96.1 304.2 %reduce-scatter.4.cloned.1.call-start = ((), (), s32[]{:S(2)}) async-start(), calls=%async_computation.3 | async-start | bytes 15138816
  100.0 123.7 %copy-start = (bf16[128,4096]{1,0:T(8,128)(2,1)S(1)}, bf16[128,4096]{1,0:T(8,128)(2,1)}, u32[]{:S(2)}) copy-start(bf16[128,4096]{1,0:T(8,128)(2,1)} %all-gather.5.cloned.1.call-done) | copy-start | bytes 3145732
Sparse Core Ops, SparseCore 0:
  9.8 40.6 all-gather.4
  96.2 92.9 all-gather.2
  250.0 150.1 reduce-scatter.3
where the time goes:
time: 411 us; the launch traced here: 409 us
  blocking collectives  182 us (44%)
  waiting for transfers between devices  166 us (40%)
  local copies, waits for them, and re-layouts  25 us (6%)
  matrix products  15 us (4%)
  between operations  14.5 us (4%)
  other arithmetic  6.28 us (2%)
    all_gather x1, waiting for transfers between devices, body(): lax.all_gather(tangent, 'dp', axis=0, tiled=True)  89.2 us
    psum x1, blocking collectives, body(): total_sq = lax.psum(jnp.sum(grad * grad), ('dp', 'tensor')) + NORM_EPSILON  81.7 us
    unnamed x4, waiting for transfers between devices  77 us
    psum x1, blocking collectives, body(): source_grad = lax.psum(local_sums, 'dp') / total_tokens  73.6 us
    psum x1, blocking collectives, body(): per_tok = lax.psum(per_tok, 'tensor')  26.8 us
    unnamed x12, local copies, waits for them, and re-layouts  25 us
  transfers between devices with their start and end apart: 3, of which 2 were waited for; matrix products, arithmetic and copies ran while one was open for 2% of the time, Pallas kernels for 0%

commit v1 on v0

v1 whole, which is shorter than its diff:
```python
import jax
import jax.numpy as jnp
from jax import lax
from jax.experimental import pallas as pl
from jax.experimental.pallas import tpu as pltpu
from jax.sharding import PartitionSpec as P

CLIP_NORM = 1.0
LEARN_RATE = 0.00015
BETA_ONE = 0.9
BETA_TWO = 0.95
ADAM_EPSILON = 1e-08
NORM_EPSILON = 1e-06

MESH = pl.DeviceIdType.MESH
BF16 = jnp.bfloat16
F32 = jnp.float32

ROWS = 128
COLS = 1792
PART = 448
TOK = 512
TOKENS = 4096
NSRC = 64


class Slots:
    def __init__(self):
        self.used = 0

    def take(self, count):
        first = self.used
        self.used += count
        return first


SLOTS = Slots()
TZ = SLOTS.take(7)
TY = SLOTS.take(24)
XZ = SLOTS.take(4)
XX = SLOTS.take(12)
XC = SLOTS.take(16)
AZ = SLOTS.take(4)
IZ = SLOTS.take(4)
N1 = SLOTS.take(24)
CC = SLOTS.take(16)
RX = SLOTS.take(12)
RZ = SLOTS.take(4)
N2 = SLOTS.take(24)
N_SEMS = SLOTS.used


def kernel(
    tokens, gate, up, hid, ids, weight, grad, mom, sec, adj,
    out, src_out,
    grad_v, mom_v, sec_v, adj_v, gate_v, up_v, hid_v,
    tok, tang, xb, acts, act, idb, norm1, norm2, proj, mixed, cb, cr, s0, s1, s2, r0, r1, r2, fin, res,
    ls, ss, rs,
):
    dp, tn = lax.axis_index("dp"), lax.axis_index("tensor")
    zh, x, c = lax.div(dp, 8), lax.rem(lax.div(dp, 2), 4), lax.rem(dp, 2)
    zl, y = lax.div(tn, 4), lax.rem(tn, 4)
    z = zh * 2 + zl
    way = 1 - 2 * c

    def dev(z_at, x_at, y_at, c_at):
        return (lax.div(z_at, 2) * 8 + x_at * 2 + c_at, lax.rem(z_at, 2) * 4 + y_at)

    def zs(k):
        return lax.rem(z + k * way + 8, 8)

    def xs(k):
        return lax.rem(x + k * way + 4, 4)

    def ys(k):
        return lax.rem(y + k * way + 4, 4)

    def zhs(k):
        return lax.rem(zh + k + 4, 4)

    def at_zh(zh_at):
        return (zh_at * 8 + x * 2 + c, tn)

    x_dev = {k: dev(z, xs(k), y, c) for k in (1, -1)}
    y_dev = {k: dev(z, x, ys(k), c) for k in (1, -1)}
    z_dev = {k: dev(zs(k), x, y, c) for k in (1, -1)}
    core = dev(z, x, y, 1 - c)

    groups = (
        [(d, dev(z, lax.div(lax.rem(x * 2 + c + d, 8), 2), y, lax.rem(c + d, 2))) for d in range(1, 8)],
        [(d, dev(z, x, lax.rem(y + d, 4), c)) for d in range(1, 4)],
        [(d, dev(lax.rem(z + d, 8), x, y, c)) for d in range(1, 8)],
    )
    places = ((x * 2 + c, 8), (y, 4), (z, 8))

    sent = []

    def push(src, dst, sem, to):
        copy = pltpu.make_async_remote_copy(
            src_ref=src, dst_ref=dst, send_sem=ss.at[sem], recv_sem=rs.at[sem], device_id=to, device_id_type=MESH
        )
        copy.start()
        sent.append(copy)

    def arrived(dst, sem):
        pltpu.make_async_remote_copy(
            src_ref=dst, dst_ref=dst, send_sem=ss.at[sem], recv_sem=rs.at[sem], device_id=core, device_id_type=MESH
        ).wait_recv()

    local = []

    def fetch(src, dst):
        copy = pltpu.make_async_copy(src, dst, ls.at[len(local)])
        copy.start()
        local.append(copy)
        return copy

    def shard(z_at, y_at):
        block = lax.rem(z_at, 2) * 4 + y_at
        return tok.at[pl.ds(2 * block, 2), pl.ds(pl.multiple_of(lax.div(z_at, 2) * ROWS, ROWS), ROWS), :]

    def spread(buf, sems, stage, value):
        place, size = places[stage]
        buf[stage, place] = value
        for d, to in groups[stage]:
            push(buf.at[stage, place], buf.at[stage, place], sems + stage * 8 + d, to)

    def collect(buf, sems, stage):
        place, size = places[stage]
        for d in range(1, size):
            arrived(buf.at[stage, lax.rem(place + size - d, size)], sems + stage * 8 + d)
        total = buf[stage, 0]
        for k in range(1, size):
            total = total + buf[stage, k]
        return total

    get_grad = fetch(grad, grad_v)
    block = zl * 4 + y
    own_rows = pl.ds(pl.multiple_of(zh * ROWS, ROWS), ROWS)
    get_tok = [
        fetch(tokens.at[:, pl.ds(h * 256, 256)], tok.at[2 * block + h, own_rows, :]) for h in range(2)
    ]
    get_acts = [fetch(gate, gate_v), fetch(up, up_v), fetch(hid, hid_v)]
    get_rest = [fetch(mom, mom_v), fetch(sec, sec_v), fetch(adj, adj_v)]

    barrier = pltpu.get_barrier_semaphore()
    n_partners = 0
    for group in groups:
        for _, to in group:
            pl.semaphore_signal(barrier, inc=1, device_id=to, device_id_type=MESH)
            n_partners += 1
    pl.semaphore_wait(barrier, n_partners)

    get_grad.wait()

    def square(k, total):
        part = grad_v[pl.ds(pl.multiple_of(k * 8, 8), 8), :]
        part = part * part
        for j in range(COLS // 128):
            total = total + part[:, j * 128 : (j + 1) * 128]
        return total

    spread(norm1, N1, 0, lax.fori_loop(0, ROWS // 8, square, jnp.zeros((8, 128), F32)))

    for copy in get_tok:
        copy.wait()

    def pass_y(m, z_at):
        here = shard(z_at, y)
        push(here, here, TY + m, y_dev[1])
        push(here, here, TY + 8 + m, y_dev[-1])

    def relay_y(m, z_at):
        there = shard(z_at, ys(-1))
        arrived(there, TY + m)
        push(there, there, TY + 16 + m, y_dev[1])

    own = shard(z, y)
    push(own, own, TZ, z_dev[1])
    push(own, own, TZ + 4, z_dev[-1])
    pass_y(0, z)

    for copy in get_acts:
        copy.wait()
    ids_row = ids[...]
    weight_row = jnp.zeros((1, ROWS), F32)
    for k in range(NSRC):
        weight_row = jnp.where(ids_row == k, weight[k], weight_row)
    weight_row = weight_row / TOKENS
    idb[zh] = jnp.broadcast_to(ids_row.astype(F32), (8, ROWS))

    def activation(j, carry):
        cols = pl.ds(pl.multiple_of(j * 128, 128), 128)
        pre = gate_v[:, cols].astype(F32)
        sigma = 1.0 / (1.0 + jnp.exp(-pre))
        coupling = up_v[:, cols].astype(F32) * hid_v[:, cols].astype(F32)
        first = coupling * sigma * (1.0 + pre * (1.0 - sigma))
        second = coupling * sigma * (1.0 - sigma) * (2.0 + pre * (1.0 - 2.0 * sigma))
        acts[0, cols, :] = first.T.astype(BF16)
        acts[1, cols, :] = (second.T * weight_row).astype(BF16)
        return carry

    lax.fori_loop(0, COLS // 128, activation, 0)

    spread(norm1, N1, 1, collect(norm1, N1, 0))

    def forward_z(k):
        z_at = zs(-k)
        arrived(shard(z_at, y), TZ + k - 1)
        if k < 4:
            push(shard(z_at, y), shard(z_at, y), TZ + k, z_dev[1])
        pass_y(2 * k - 1, z_at)

    def backward_z(k):
        z_at = zs(k)
        arrived(shard(z_at, y), TZ + 4 + k - 1)
        if k < 3:
            push(shard(z_at, y), shard(z_at, y), TZ + 4 + k, z_dev[-1])
        pass_y(2 * k, z_at)

    forward_z(1)
    backward_z(1)
    spread(norm1, N1, 2, collect(norm1, N1, 1))
    relay_y(0, z)
    forward_z(2)
    backward_z(2)

    total_sq = jnp.sum(collect(norm1, N1, 2), keepdims=True) + NORM_EPSILON
    clip = jnp.minimum(CLIP_NORM * lax.rsqrt(total_sq), 1.0)
    for copy in get_rest:
        copy.wait()

    def tangent(j, carry):
        cols = pl.ds(pl.multiple_of(j * 128, 128), 128)
        clipped = clip * grad_v[:, cols]
        moment_new = BETA_ONE * mom_v[:, cols] + (1.0 - BETA_ONE) * clipped
        second_new = BETA_TWO * sec_v[:, cols] + (1.0 - BETA_TWO) * clipped * clipped
        root_v = jnp.sqrt(second_new)
        inverse = 1.0 / (root_v + ADAM_EPSILON)
        jacobian = -LEARN_RATE * (
            (1.0 - BETA_ONE) * inverse - moment_new * (1.0 - BETA_TWO) * clipped * (inverse * inverse / root_v)
        )
        pulled = jacobian * adj_v[:, cols]
        tang[cols, :] = (clip * pulled).T.astype(BF16)
        return carry

    lax.fori_loop(0, COLS // 128, tangent, 0)

    def part_rows(q):
        return pl.ds(pl.multiple_of(q * PART, 64), PART)

    keep = fetch(tang.at[part_rows(zh), :], xb.at[dp])
    for d in (2, 1, 3):
        push(tang.at[part_rows(zhs(d)), :], xb.at[dp], XZ + d, at_zh(zhs(d)))

    relay_y(1, zs(-1))
    relay_y(2, zs(1))
    forward_z(3)
    backward_z(3)
    relay_y(3, zs(-2))
    relay_y(4, zs(2))
    forward_z(4)

    def x_block(x_at, d):
        return xb.at[zhs(-d) * 8 + x_at * 2 + c]

    def to_core(x_at, offset, d):
        push(x_block(x_at, d), x_block(x_at, d), XC + offset * 4 + d, core)

    keep.wait()
    for d in (0, 1, 3, 2):
        here = x_block(x, d)
        if d:
            arrived(here, XZ + d)
        push(here, here, XX + d, x_dev[1])
        push(here, here, XX + 4 + d, x_dev[-1])
        to_core(x, 0, d)

    for d in (1, 3, 2):
        to = at_zh(zhs(d))
        push(acts.at[:, part_rows(zhs(d)), :], act.at[zh], AZ + d, to)
        push(idb.at[zh], idb.at[zh], IZ + d, to)
    keep_act = fetch(acts.at[:, part_rows(zh), :], act.at[zh])

    behind, ahead = 3 - 2 * c, 1 + 2 * c
    relay_y(5, zs(-3))
    relay_y(6, zs(3))
    for d in (0, 1, 3, 2):
        there = x_block(xs(-1), d)
        arrived(there, XX + d)
        push(there, there, XX + 8 + d, x_dev[1])
        to_core(xs(-1), behind, d)
        there = x_block(xs(1), d)
        arrived(there, XX + 4 + d)
        to_core(xs(1), ahead, d)
    relay_y(7, zs(-4))
    for d in (0, 1, 3, 2):
        there = x_block(xs(2), d)
        arrived(there, XX + 8 + d)
        to_core(xs(2), 2, d)

    offsets = [z] + [zs(k) for k in (-1, 1, -2, 2, -3, 3, -4)]
    for m, z_at in enumerate(offsets):
        arrived(shard(z_at, ys(1)), TY + 8 + m)
    for m, z_at in enumerate(offsets):
        arrived(shard(z_at, ys(2)), TY + 16 + m)
    for offset in range(4):
        for d in range(4):
            arrived(xb.at[zhs(-d) * 8 + lax.rem(x + offset, 4) * 2 + 1 - c], XC + offset * 4 + d)

    proj[...] = jnp.zeros_like(proj)

    def first_product(k, carry):
        left = jnp.concatenate([xb[8 * k + i] for i in range(8)], axis=1)
        right = jnp.concatenate([tok[4 * k + i] for i in range(4)], axis=1)
        proj[...] += lax.dot_general(left, right, (((1,), (1,)), ((), ())), preferred_element_type=F32)
        return carry

    lax.fori_loop(0, 4, first_product, 0)

    keep_act.wait()
    for d in (1, 3, 2):
        arrived(act.at[zhs(-d)], AZ + d)
        arrived(idb.at[zhs(-d)], IZ + d)

    sums = jnp.zeros((8, 128), F32)
    source = lax.broadcasted_iota(jnp.int32, (128, ROWS), 0).astype(F32)
    for k in range(4):
        cols = pl.ds(k * ROWS, ROWS)
        part = proj[:, cols]
        mixed[:, cols] = (part * act[k, 1].astype(F32)).astype(BF16)
        per_tok = jnp.sum(part * act[k, 0].astype(F32), axis=0, keepdims=True)
        onehot = (source == idb[k, 0:1, :]).astype(F32)
        sums = sums + lax.dot_general(
            jnp.broadcast_to(per_tok, (8, ROWS)),
            onehot,
            (((1,), (1,)), ((), ())),
            precision=lax.Precision.HIGHEST,
            preferred_element_type=F32,
        )
    order = (2, 1, 3, 0)

    def second_product(x_at, zh_at):
        whole = jnp.dot(mixed[...], tok[zh_at * 4 + x_at], preferred_element_type=F32)
        cb[x_at, zh_at, 0] = whole[:, :128].astype(BF16)
        cb[x_at, zh_at, 1] = whole[:, 128:].astype(BF16)

    def products(j):
        zh_at = zhs(order[j])
        for offset in (2, behind, ahead, 0):
            x_at = lax.rem(x + offset, 4)
            second_product(x_at, zh_at)
            push(cb.at[x_at, zh_at, 1 - c], cr.at[x_at, zh_at], CC + offset * 4 + j, core)

    def both(offset, j):
        x_at, zh_at = lax.rem(x + offset, 4), zhs(order[j])
        arrived(cr.at[x_at, zh_at], CC + offset * 4 + j)
        return cb[x_at, zh_at, c].astype(F32) + cr[x_at, zh_at].astype(F32)

    def outward(j):
        s0[j] = both(2, j).astype(BF16)
        push(s0.at[j], r0.at[j], RX + j, x_dev[1])
        s2[j] = both(behind, j).astype(BF16)
        push(s2.at[j], r2.at[j], RX + 8 + j, x_dev[-1])

    def onward(j):
        part = both(ahead, j)
        arrived(r0.at[j], RX + j)
        s1[j] = (part + r0[j].astype(F32)).astype(BF16)
        push(s1.at[j], r1.at[j], RX + 4 + j, x_dev[1])

    def finish(j):
        part = both(0, j)
        arrived(r2.at[j], RX + 8 + j)
        part = part + r2[j].astype(F32)
        arrived(r1.at[j], RX + 4 + j)
        fin[j] = (part + r1[j].astype(F32)).astype(BF16)
        d = order[j]
        if d:
            push(fin.at[j], res.at[part_rows(zh), :], RZ + d, at_zh(zhs(d)))
        else:
            res[part_rows(zh), :] = fin[j]

    products(0)
    products(1)
    outward(0)
    products(2)
    outward(1)
    products(3)
    outward(2)
    outward(3)
    spread(norm2, N2, 0, sums)
    onward(0)
    onward(1)
    spread(norm2, N2, 1, collect(norm2, N2, 0))
    onward(2)
    onward(3)
    finish(0)
    spread(norm2, N2, 2, collect(norm2, N2, 1))
    finish(1)
    finish(2)
    finish(3)
    src_out[...] = collect(norm2, N2, 2) / TOKENS
    for d in (1, 3, 2):
        arrived(res.at[part_rows(zhs(-d)), :], RZ + d)

    def emit(j, carry):
        cols = pl.ds(pl.multiple_of(j * 128, 128), 128)
        out[:, cols] = res[cols, :].astype(F32).T
        return carry

    lax.fori_loop(0, COLS // 128, emit, 0)
    for copy in sent:
        copy.wait_send()


def body(tokens, gate_pre, up_act, hidden_cot, source_ids, data_weight, grad, moment_m, moment_v, val_adjoint):
    hbm = pl.BlockSpec(memory_space=pl.ANY)
    vmem = pl.BlockSpec(memory_space=pltpu.VMEM)
    smem = pl.BlockSpec(memory_space=pltpu.SMEM)
    curvature, sums = pl.pallas_call(
        kernel,
        name="metagradient",
        out_shape=(jax.ShapeDtypeStruct((ROWS, COLS), F32), jax.ShapeDtypeStruct((8, 128), F32)),
        in_specs=[hbm, hbm, hbm, hbm, vmem, smem, hbm, hbm, hbm, hbm],
        out_specs=(vmem, vmem),
        scratch_shapes=[
            *[pltpu.VMEM((ROWS, COLS), F32)] * 4,
            *[pltpu.VMEM((ROWS, COLS), BF16)] * 3,
            pltpu.VMEM((16, TOK, 256), BF16),
            pltpu.VMEM((COLS, ROWS), BF16),
            pltpu.VMEM((32, PART, 128), BF16),
            pltpu.VMEM((2, COLS, ROWS), BF16),
            pltpu.VMEM((4, 2, PART, ROWS), BF16),
            pltpu.VMEM((4, 8, ROWS), F32),
            pltpu.VMEM((3, 8, 8, 128), F32),
            pltpu.VMEM((3, 8, 8, 128), F32),
            pltpu.VMEM((PART, TOK), F32),
            pltpu.VMEM((PART, TOK), BF16),
            pltpu.VMEM((4, 4, 2, PART, 128), BF16),
            pltpu.VMEM((4, 4, PART, 128), BF16),
            *[pltpu.VMEM((4, PART, 128), BF16)] * 7,
            pltpu.VMEM((COLS, ROWS), BF16),
            pltpu.SemaphoreType.DMA((12,)),
            pltpu.SemaphoreType.DMA((N_SEMS,)),
            pltpu.SemaphoreType.DMA((N_SEMS,)),
        ],
        compiler_params=pltpu.CompilerParams(
            collective_id=0, has_side_effects=True, vmem_limit_bytes=60 * 2**20
        ),
    )(
        tokens,
        gate_pre,
        up_act,
        hidden_cot,
        source_ids.reshape(1, ROWS),
        data_weight,
        grad,
        moment_m,
        moment_v,
        val_adjoint,
    )
    return curvature, sums[0, :NSRC]


def solution(mesh):
    split = P("dp", "tensor")
    in_specs = (split, split, split, split, P("dp"), P(), split, split, split, split)
    return jax.shard_map(body, mesh=mesh, in_specs=in_specs, out_specs=(split, P()), check_vma=False)
```

time: 411 us -> 101 us (0.25)
  blocking collectives: 182 us -> 0 us
  waiting for transfers between devices: 166 us -> 0 us
  Pallas kernels: 0 us -> 96.7 us
  local copies, waits for them, and re-layouts: 25 us -> 3.35 us
  matrix products: 15 us -> 0 us
  between operations: 14.5 us -> 0.64 us
  other arithmetic: 6.28 us -> 0 us
    psum x3 -> x0, blocking collectives: 182 us -> none  [the longest x1 81.7 us: body(): total_sq = lax.psum(jnp.sum(grad * grad), ('dp', 'tensor')) + NORM_EPSILON]
    pallas_call x0 -> x1, Pallas kernels: none -> 96.7 us  [body(): pl.pallas_call(kernel, name='metagradient', out_shape=(jax.ShapeDtypeStru...]
    all_gather x2 -> x0, waiting for transfers between devices: 89.2 us -> none  [the longest x1 89.2 us: body(): lax.all_gather(tangent, 'dp', axis=0, tiled=True)]
    unnamed x4 -> x0, waiting for transfers between devices: 77 us -> none
    unnamed x12 -> x1, local copies, waits for them, and re-layouts: 25 us -> 2.16 us
    dot_general x2 -> x0, matrix products: 15 us -> none  [the longest x1 7.59 us: body(): jnp.dot(token_cols, lax.all_gather(tangent, 'dp', axis=0, tiled=True), pr...]
  transfers between devices with their start and end apart: 3 -> 0, of which waited for: 2 -> 0; matrix products, arithmetic and copies ran while one was open for 2% -> 0% of each run, Pallas kernels for 0% -> 0%
where the time goes in v1:
time: 101 us
  Pallas kernels  96.7 us (96%)
  local copies, waits for them, and re-layouts  3.35 us (3%)
    pallas_call x1, Pallas kernels, body(): pl.pallas_call(kernel, name='metagradient', out_shape=(jax.ShapeDtypeStru...  96.7 us
    unnamed x1, local copies, waits for them, and re-layouts  2.16 us

profile of v1, /device:TPU:1, one launch (start us, length us, event | category | flops | bytes accessed | tf_op | source)
XLA Modules:
  0.0 100.7 jit_solution(13513729427403302521)
XLA Ops:
  0.6 96.7 %metagradient.1 = (f32[128,1792]{1,0:T(8,128)}, f32[8,128]{1,0:T(8,128)}) custom-call(bf16[128,512]{1,0:T(8,128)(2,1)} %tokens.1, bf16[128,1792]{1,0:T(8,128)(2,1)} %gate.1, bf16[128,1792]{1,0:T(8,128)(2,1)} %up.1, bf16[128,1792]{1,0:T(8,128)(2,1)} %hid.1, s32[1,128]{1,0:T(1,128)} %bitcast.3, f32[64]{0:T(128)} %weight.1, f32[128,1792]{1,0:T(8,128)} %grad.1, ...), custom_call_target="tpu_custom_call" | custom-call | tf_op jit(solution)/shard_map/metagradient/pallas_call | solution.py:421
  97.4 1.2 %slice_bitcast_fusion = f32[64]{0:T(128)} fusion(f32[8,128]{1,0:T(8,128)} %get-tuple-element.5), kind=kLoop, calls=%fused_computation | loop fusion | bytes 512 | tf_op jit(solution)/shard_map/squeeze | solution.py:463
  98.6 2.2 %copy.13 = f32[128,1792]{1,0:T(8,128)} copy(f32[128,1792]{1,0:T(8,128)} %get-tuple-element.8) | data formatting | bytes 1835008

commit v2 on v1

v2 whole, which is shorter than its diff:
```python
import contextlib

import jax
import jax.numpy as jnp
from jax import lax
from jax.experimental import pallas as pl
from jax.experimental.pallas import tpu as pltpu
from jax.sharding import PartitionSpec as P

CLIP_NORM = 1.0
LEARN_RATE = 0.00015
BETA_ONE = 0.9
BETA_TWO = 0.95
ADAM_EPSILON = 1e-08
NORM_EPSILON = 1e-06

MESH = pl.DeviceIdType.MESH
BF16 = jnp.bfloat16
F32 = jnp.float32

ROWS = 128
COLS = 1792
PART = 448
TOK = 512
TOKENS = 4096
NSRC = 64


def mark(name):
    return contextlib.nullcontext()


class Slots:
    def __init__(self):
        self.used = 0

    def take(self, count):
        first = self.used
        self.used += count
        return first


RECV = Slots()
TZ = RECV.take(7)
TY = RECV.take(8)
TY_AHEAD = RECV.take(1)
TY_RELAY = RECV.take(1)
XZ = RECV.take(4)
XX = RECV.take(12)
XC = RECV.take(1)
AZ = RECV.take(2)
IZ = RECV.take(1)
N1 = RECV.take(3)
CC = RECV.take(16)
RX = RECV.take(12)
RZ = RECV.take(1)
N2 = RECV.take(3)
SEND = Slots()
S_TZ = SEND.take(1)
S_TY = SEND.take(1)
S_X = SEND.take(1)
S_A = SEND.take(2)
S_I = SEND.take(1)
S_N1 = SEND.take(3)
S_CC = SEND.take(1)
S_R = SEND.take(1)
S_Z = SEND.take(1)
S_N2 = SEND.take(3)


def kernel(
    tokens, gate, up, hid, ids, weight, grad, mom, sec, adj,
    res, src_out,
    grad_v, mom_v, sec_v, adj_v, gate_v, up_v, hid_v,
    tok, tang, xb, acts, act, idb, norm1, norm2, proj, mixed, cb, cr, s0, s1, s2, r0, r1, r2, fin,
    ls, ss, rs,
):
    dp, tn = lax.axis_index("dp"), lax.axis_index("tensor")
    zh, x, c = lax.div(dp, 8), lax.rem(lax.div(dp, 2), 4), lax.rem(dp, 2)
    zl, y = lax.div(tn, 4), lax.rem(tn, 4)
    z = zh * 2 + zl
    way = 1 - 2 * c

    def dev(z_at, x_at, y_at, c_at):
        return (lax.div(z_at, 2) * 8 + x_at * 2 + c_at, lax.rem(z_at, 2) * 4 + y_at)

    def zs(k):
        return lax.rem(z + k * way + 8, 8)

    def xs(k):
        return lax.rem(x + k * way + 4, 4)

    def ys(k):
        return lax.rem(y + k * way + 4, 4)

    def zhs(k):
        return lax.rem(zh + k + 4, 4)

    def at_zh(zh_at):
        return (zh_at * 8 + x * 2 + c, tn)

    x_dev = {k: dev(z, xs(k), y, c) for k in (1, -1)}
    y_dev = {k: dev(z, x, ys(k), c) for k in (1, -1)}
    z_dev = {k: dev(zs(k), x, y, c) for k in (1, -1)}
    core = dev(z, x, y, 1 - c)

    groups = (
        [dev(z, x, lax.rem(y + d, 4), c) for d in range(1, 4)],
        [dev(lax.rem(z + d, 8), x, y, c) for d in range(1, 8)],
        [dev(z, lax.div(lax.rem(x * 2 + c + d, 8), 2), y, lax.rem(c + d, 2)) for d in range(1, 8)],
    )
    places = (y, z, x * 2 + c)

    def push(src, dst, send, recv, to):
        pltpu.make_async_remote_copy(
            src_ref=src, dst_ref=dst, send_sem=ss.at[send], recv_sem=rs.at[recv], device_id=to, device_id_type=MESH
        ).start()

    def counted(ref, send, recv):
        return pltpu.make_async_remote_copy(
            src_ref=ref, dst_ref=ref, send_sem=ss.at[send], recv_sem=rs.at[recv], device_id=core, device_id_type=MESH
        )

    def arrived(ref, recv):
        counted(ref, 0, recv).wait_recv()

    def drained(ref, send):
        counted(ref, send, 0).wait_send()

    local = []

    def fetch(src, dst):
        copy = pltpu.make_async_copy(src, dst, ls.at[len(local)])
        copy.start()
        local.append(copy)
        return copy

    def shard(z_at, y_at):
        block = lax.rem(z_at, 2) * 4 + y_at
        return tok.at[pl.ds(2 * block, 2), pl.ds(pl.multiple_of(lax.div(z_at, 2) * ROWS, ROWS), ROWS), :]

    def spread(buf, send, recv, stage, value):
        place = places[stage]
        buf[stage, place] = value
        for to in groups[stage]:
            push(buf.at[stage, place], buf.at[stage, place], send + stage, recv + stage, to)

    def collect(buf, recv, stage):
        size = len(groups[stage]) + 1
        arrived(buf.at[stage, pl.ds(0, size - 1)], recv + stage)
        total = buf[stage, 0]
        for k in range(1, size):
            total = total + buf[stage, k]
        return total

    get_grad = fetch(grad, grad_v)
    block = zl * 4 + y
    own_rows = pl.ds(pl.multiple_of(zh * ROWS, ROWS), ROWS)
    get_tok = [fetch(tokens.at[:, pl.ds(h * 256, 256)], tok.at[2 * block + h, own_rows, :]) for h in range(2)]
    get_acts = [fetch(gate, gate_v), fetch(up, up_v), fetch(hid, hid_v)]
    get_rest = [fetch(mom, mom_v), fetch(sec, sec_v), fetch(adj, adj_v)]

    with mark("barrier"):
        barrier = pltpu.get_barrier_semaphore()
        for group in groups:
            for to in group:
                pl.semaphore_signal(barrier, inc=1, device_id=to, device_id_type=MESH)
        pl.semaphore_wait(barrier, sum(len(group) for group in groups))

    get_grad.wait()

    def square(k, total):
        part = grad_v[pl.ds(pl.multiple_of(k * 8, 8), 8), :]
        part = part * part
        for j in range(COLS // 128):
            total = total + part[:, j * 128 : (j + 1) * 128]
        return total

    with mark("squares"):
        spread(norm1, S_N1, N1, 0, lax.fori_loop(0, ROWS // 8, square, jnp.zeros((8, 128), F32)))

    for copy in get_tok:
        copy.wait()

    def pass_y(m, z_at):
        here = shard(z_at, y)
        push(here, here, S_TY, TY + m, y_dev[1])
        push(here, here, S_TY, TY_AHEAD, y_dev[-1])

    def relay_y(m, z_at):
        with mark(f"ry{m}"):
            there = shard(z_at, ys(-1))
            arrived(there, TY + m)
            push(there, there, S_TY, TY_RELAY, y_dev[1])

    own = shard(z, y)
    push(own, own, S_TZ, TZ, z_dev[1])
    push(own, own, S_TZ, TZ + 4, z_dev[-1])
    pass_y(0, z)

    for copy in get_acts:
        copy.wait()
    ids_row = ids[...]
    weight_row = jnp.zeros((1, ROWS), F32)
    for k in range(NSRC):
        weight_row = jnp.where(ids_row == k, weight[k], weight_row)
    weight_row = weight_row / TOKENS
    idb[zh] = jnp.broadcast_to(ids_row.astype(F32), (8, ROWS))

    def activation(j, carry):
        cols = pl.ds(pl.multiple_of(j * 128, 128), 128)
        pre = gate_v[:, cols].astype(F32)
        sigma = 1.0 / (1.0 + jnp.exp(-pre))
        coupling = up_v[:, cols].astype(F32) * hid_v[:, cols].astype(F32)
        first = coupling * sigma * (1.0 + pre * (1.0 - sigma))
        second = coupling * sigma * (1.0 - sigma) * (2.0 + pre * (1.0 - 2.0 * sigma))
        acts[0, cols, :] = first.T.astype(BF16)
        acts[1, cols, :] = (second.T * weight_row).astype(BF16)
        return carry

    with mark("activation"):
        lax.fori_loop(0, COLS // 128, activation, 0)

    def part_rows(q):
        return pl.ds(pl.multiple_of(q * PART, 64), PART)

    def share_acts(which):
        for d in (2, 1, 3):
            push(acts.at[which, part_rows(zhs(d)), :], act.at[which, zh], S_A + which, AZ + which, at_zh(zhs(d)))

    for d in (1, 2, 3):
        push(idb.at[zh], idb.at[zh], S_I, IZ, at_zh(zhs(d)))
    keep_act = [fetch(acts.at[k, part_rows(zh), :], act.at[k, zh]) for k in range(2)]

    with mark("norm_a"):
        spread(norm1, S_N1, N1, 1, collect(norm1, N1, 0))

    def forward_z(k):
        with mark(f"fz{k}"):
            z_at = zs(-k)
            arrived(shard(z_at, y), TZ + k - 1)
            if k < 4:
                push(shard(z_at, y), shard(z_at, y), S_TZ, TZ + k, z_dev[1])
            pass_y(2 * k - 1, z_at)

    def backward_z(k):
        with mark(f"bz{k}"):
            z_at = zs(k)
            arrived(shard(z_at, y), TZ + 4 + k - 1)
            if k < 3:
                push(shard(z_at, y), shard(z_at, y), S_TZ, TZ + 4 + k, z_dev[-1])
            pass_y(2 * k, z_at)

    forward_z(1)
    backward_z(1)
    with mark("norm_b"):
        spread(norm1, S_N1, N1, 2, collect(norm1, N1, 1))
    relay_y(0, z)
    forward_z(2)
    backward_z(2)
    with mark("norm_c"):
        total_sq = jnp.sum(collect(norm1, N1, 2), keepdims=True) + NORM_EPSILON
    clip = jnp.minimum(CLIP_NORM * lax.rsqrt(total_sq), 1.0)
    for copy in get_rest:
        copy.wait()

    def tangent(j, carry):
        cols = pl.ds(pl.multiple_of(j * 128, 128), 128)
        clipped = clip * grad_v[:, cols]
        moment_new = BETA_ONE * mom_v[:, cols] + (1.0 - BETA_ONE) * clipped
        second_new = BETA_TWO * sec_v[:, cols] + (1.0 - BETA_TWO) * clipped * clipped
        root_v = jnp.sqrt(second_new)
        inverse = 1.0 / (root_v + ADAM_EPSILON)
        jacobian = -LEARN_RATE * (
            (1.0 - BETA_ONE) * inverse - moment_new * (1.0 - BETA_TWO) * clipped * (inverse * inverse / root_v)
        )
        pulled = jacobian * adj_v[:, cols]
        tang[cols, :] = (clip * pulled).T.astype(BF16)
        return carry

    with mark("tangent"):
        lax.fori_loop(0, COLS // 128, tangent, 0)

    keep = fetch(tang.at[part_rows(zh), :], xb.at[dp])
    forward_z(3)
    backward_z(3)
    for d in (1, 3, 2):
        push(tang.at[part_rows(zhs(d)), :], xb.at[dp], S_X, XZ + d, at_zh(zhs(d)))

    def x_block(x_at, d):
        return xb.at[zhs(-d) * 8 + x_at * 2 + c]

    def x_own(d):
        with mark(f"xown{d}"):
            here = x_block(x, d)
            if d:
                arrived(here, XZ + d)
            else:
                keep.wait()
            push(here, here, S_X, XX + d, x_dev[1])
            push(here, here, S_X, XX + 4 + d, x_dev[-1])
            push(here, here, S_X, XC, core)

    def x_sides(d):
        with mark(f"xside{d}"):
            there = x_block(xs(-1), d)
            arrived(there, XX + d)
            push(there, there, S_X, XX + 8 + d, x_dev[1])
            push(there, there, S_X, XC, core)
            there = x_block(xs(1), d)
            arrived(there, XX + 4 + d)
            push(there, there, S_X, XC, core)

    def x_relay(d):
        with mark(f"xrelay{d}"):
            there = x_block(xs(2), d)
            arrived(there, XX + 8 + d)
            push(there, there, S_X, XC, core)

    x_own(0)
    relay_y(1, zs(-1))
    relay_y(2, zs(1))
    x_sides(0)
    relay_y(3, zs(-2))
    forward_z(4)
    x_own(1)
    x_own(3)
    x_relay(0)
    relay_y(4, zs(2))
    x_own(2)
    share_acts(1)
    share_acts(0)
    x_sides(1)
    x_sides(3)
    relay_y(5, zs(-3))
    x_relay(1)
    x_relay(3)
    x_sides(2)
    relay_y(6, zs(3))
    x_relay(2)
    relay_y(7, zs(-4))

    with mark("ylast"):
        arrived(tok.at[pl.ds(0, 4)], TY_AHEAD)
        arrived(tok.at[pl.ds(0, 4)], TY_RELAY)
    with mark("xcore"):
        arrived(xb.at[pl.ds(0, 16)], XC)

    proj[...] = jnp.zeros_like(proj)

    def first_product(k, carry):
        left = jnp.concatenate([xb[8 * k + i] for i in range(8)], axis=1)
        right = jnp.concatenate([tok[4 * k + i] for i in range(4)], axis=1)
        proj[...] += lax.dot_general(left, right, (((1,), (1,)), ((), ())), preferred_element_type=F32)
        return carry

    with mark("product1"):
        lax.fori_loop(0, 4, first_product, 0)

    with mark("second_wait"):
        for copy in keep_act:
            copy.wait()
        arrived(act.at[1, pl.ds(0, 3)], AZ + 1)

    with mark("mix"):
        for k in range(4):
            cols = pl.ds(k * ROWS, ROWS)
            mixed[:, cols] = (proj[:, cols] * act[1, k].astype(F32)).astype(BF16)

    def source_sums():
        arrived(act.at[0, pl.ds(0, 3)], AZ)
        arrived(idb.at[pl.ds(0, 3)], IZ)
        sums = jnp.zeros((8, 128), F32)
        source = lax.broadcasted_iota(jnp.int32, (128, ROWS), 0).astype(F32)
        for k in range(4):
            part = proj[:, pl.ds(k * ROWS, ROWS)]
            per_tok = jnp.sum(part * act[0, k].astype(F32), axis=0, keepdims=True)
            onehot = (source == idb[k, 0:1, :]).astype(F32)
            sums = sums + lax.dot_general(
                jnp.broadcast_to(per_tok, (8, ROWS)),
                onehot,
                (((1,), (1,)), ((), ())),
                precision=lax.Precision.HIGHEST,
                preferred_element_type=F32,
            )
        return sums

    order = (2, 1, 3, 0)
    behind, ahead = 3 - 2 * c, 1 + 2 * c

    def second_product(offset, j):
        x_at, zh_at = lax.rem(x + offset, 4), zhs(order[j])
        whole = jnp.dot(mixed[...], tok[zh_at * 4 + x_at], preferred_element_type=F32)
        cb[x_at, zh_at, 0] = whole[:, :128].astype(BF16)
        cb[x_at, zh_at, 1] = whole[:, 128:].astype(BF16)
        push(cb.at[x_at, zh_at, 1 - c], cr.at[x_at, zh_at], S_CC, CC + offset * 4 + j, core)

    def both(offset, j):
        x_at, zh_at = lax.rem(x + offset, 4), zhs(order[j])
        arrived(cr.at[x_at, zh_at], CC + offset * 4 + j)
        return cb[x_at, zh_at, c].astype(F32) + cr[x_at, zh_at].astype(F32)

    def opposite(j):
        with mark(f"opposite{j}"):
            s0[j] = both(2, j).astype(BF16)
            push(s0.at[j], r0.at[j], S_R, RX + j, x_dev[1])

    def backward(j):
        with mark(f"backward{j}"):
            s2[j] = both(behind, j).astype(BF16)
            push(s2.at[j], r2.at[j], S_R, RX + 8 + j, x_dev[-1])

    def onward(j):
        with mark(f"onward{j}"):
            part = both(ahead, j)
            arrived(r0.at[j], RX + j)
            s1[j] = (part + r0[j].astype(F32)).astype(BF16)
            push(s1.at[j], r1.at[j], S_R, RX + 4 + j, x_dev[1])

    def finish(j):
        with mark(f"finish{j}"):
            part = both(0, j)
            arrived(r2.at[j], RX + 8 + j)
            part = part + r2[j].astype(F32)
            arrived(r1.at[j], RX + 4 + j)
            fin[j] = (part + r1[j].astype(F32)).astype(BF16)
            d = order[j]
            if d:
                push(fin.at[j], res.at[part_rows(zh), :], S_Z, RZ, at_zh(zhs(d)))
            else:
                fetch(fin.at[j], res.at[part_rows(zh), :])

    todo = (
        (2, 0), (1, 0), (3, 0), (2, 1), (1, 1), (3, 1), (2, 2), (0, 0), (1, 2), (3, 2), (2, 3), (0, 1), (1, 3), (3, 3), (0, 2), (0, 3),
    )
    then = {
        4: [(opposite, 0)], 6: [(backward, 0)], 7: [(opposite, 1)], 9: [(backward, 1)], 10: [(opposite, 2)],
        12: [(onward, 0)], 13: [(backward, 2)], 14: [(opposite, 3)], 15: [(onward, 1), (backward, 3)],
    }
    for i, (offset, j) in enumerate(todo):
        with mark(f"second{i}"):
            second_product(offset, j)
        for step, at in then.get(i, ()):
            step(at)
    with mark("n2_0"):
        spread(norm2, S_N2, N2, 0, source_sums())
    onward(2)
    with mark("n2_1"):
        spread(norm2, S_N2, N2, 1, collect(norm2, N2, 0))
    finish(0)
    onward(3)
    finish(1)
    with mark("n2_2"):
        spread(norm2, S_N2, N2, 2, collect(norm2, N2, 1))
    finish(2)
    finish(3)
    with mark("zlast"):
        arrived(cr.at[0, pl.ds(0, 3)], RZ)
    with mark("n2_3"):
        src_out[...] = collect(norm2, N2, 2) / TOKENS
    with mark("drain"):
        local[-1].wait()
        drained(tok.at[pl.ds(0, 7), pl.ds(0, 256)], S_TZ)
        drained(tok.at[pl.ds(0, 12)], S_TY)
        drained(xb.at[pl.ds(0, 31)], S_X)
        for which in range(2):
            drained(act.at[which, pl.ds(0, 3)], S_A + which)
        drained(idb.at[pl.ds(0, 3)], S_I)
        drained(cr, S_CC)
        drained(cr.at[pl.ds(0, 3)], S_R)
        drained(cr.at[0, pl.ds(0, 3)], S_Z)
        for stage in range(3):
            drained(norm1.at[0, pl.ds(0, len(groups[stage]))], S_N1 + stage)
            drained(norm2.at[0, pl.ds(0, len(groups[stage]))], S_N2 + stage)


def emit(res, sums, out, src):
    def turn(j, carry):
        cols = pl.ds(pl.multiple_of(j * 128, 128), 128)
        out[:, cols] = res[cols, :].astype(F32).T
        return carry

    lax.fori_loop(0, COLS // 128, turn, 0, unroll=2)
    src[...] = sums[0:1, :NSRC]


def body(tokens, gate_pre, up_act, hidden_cot, source_ids, data_weight, grad, moment_m, moment_v, val_adjoint):
    hbm = pl.BlockSpec(memory_space=pl.ANY)
    vmem = pl.BlockSpec(memory_space=pltpu.VMEM)
    smem = pl.BlockSpec(memory_space=pltpu.SMEM)
    turned, sums = pl.pallas_call(
        kernel,
        name="metagradient",
        out_shape=(jax.ShapeDtypeStruct((COLS, ROWS), BF16), jax.ShapeDtypeStruct((8, 128), F32)),
        in_specs=[hbm, hbm, hbm, hbm, vmem, smem, hbm, hbm, hbm, hbm],
        out_specs=(hbm, vmem),
        scratch_shapes=[
            *[pltpu.VMEM((ROWS, COLS), F32)] * 4,
            *[pltpu.VMEM((ROWS, COLS), BF16)] * 3,
            pltpu.VMEM((16, TOK, 256), BF16),
            pltpu.VMEM((COLS, ROWS), BF16),
            pltpu.VMEM((32, PART, 128), BF16),
            pltpu.VMEM((2, COLS, ROWS), BF16),
            pltpu.VMEM((2, 4, PART, ROWS), BF16),
            pltpu.VMEM((4, 8, ROWS), F32),
            pltpu.VMEM((3, 8, 8, 128), F32),
            pltpu.VMEM((3, 8, 8, 128), F32),
            pltpu.VMEM((PART, TOK), F32),
            pltpu.VMEM((PART, TOK), BF16),
            pltpu.VMEM((4, 4, 2, PART, 128), BF16),
            pltpu.VMEM((4, 4, PART, 128), BF16),
            *[pltpu.VMEM((4, PART, 128), BF16)] * 7,
            pltpu.SemaphoreType.DMA((14,)),
            pltpu.SemaphoreType.DMA((SEND.used,)),
            pltpu.SemaphoreType.DMA((RECV.used,)),
        ],
        compiler_params=pltpu.CompilerParams(
            collective_id=0, has_side_effects=True, vmem_limit_bytes=60 * 2**20
        ),
    )(
        tokens,
        gate_pre,
        up_act,
        hidden_cot,
        source_ids.reshape(1, ROWS),
        data_weight,
        grad,
        moment_m,
        moment_v,
        val_adjoint,
    )
    curvature, source_grad = pl.pallas_call(
        emit,
        name="emit",
        out_shape=(jax.ShapeDtypeStruct((ROWS, COLS), F32), jax.ShapeDtypeStruct((1, NSRC), F32)),
        in_specs=[vmem, vmem],
        out_specs=(vmem, vmem),
        compiler_params=pltpu.CompilerParams(vmem_limit_bytes=60 * 2**20),
    )(turned, sums)
    return curvature, source_grad.reshape(NSRC)


def solution(mesh):
    split = P("dp", "tensor")
    in_specs = (split, split, split, split, P("dp"), P(), split, split, split, split)
    return jax.shard_map(body, mesh=mesh, in_specs=in_specs, out_specs=(split, P()), check_vma=False)
```

time: 101 us -> 88.3 us (0.87)
  Pallas kernels: 96.7 us -> 87.5 us
  local copies, waits for them, and re-layouts: 3.35 us -> 0 us
    pallas_call x1, Pallas kernels: 96.7 us -> 84.8 us  [body(): pl.pallas_call(kernel, name='metagradient', out_shape=(jax.ShapeDtypeStru...]
    pallas_call x0 -> x1, Pallas kernels: none -> 2.7 us  [body(): pl.pallas_call(emit, name='emit', out_shape=(jax.ShapeDtypeStruct((ROWS,...]
    unnamed x1 -> x0, local copies, waits for them, and re-layouts: 2.16 us -> none
    squeeze x1 -> x0, local copies, waits for them, and re-layouts: 1.19 us -> none  [body(): return (curvature, sums[0, :NSRC])]
where the time goes in v2:
time: 88.3 us; the launch traced here: 88.1 us
  Pallas kernels  87.5 us (99%)
    pallas_call x1, Pallas kernels, body(): pl.pallas_call(kernel, name='metagradient', out_shape=(jax.ShapeDtypeStru...  84.8 us
    pallas_call x1, Pallas kernels, body(): pl.pallas_call(emit, name='emit', out_shape=(jax.ShapeDtypeStruct((ROWS,...  2.7 us

profile of v2, /device:TPU:1, one launch (start us, length us, event | category | flops | bytes accessed | tf_op | source)
XLA Modules:
  0.0 88.1 jit_solution(7861437274076169595)
XLA Ops:
  0.6 84.8 %metagradient.1 = (bf16[1792,128]{1,0:T(8,128)(2,1)}, f32[8,128]{1,0:T(8,128)}) custom-call(bf16[128,512]{1,0:T(8,128)(2,1)} %tokens.1, bf16[128,1792]{1,0:T(8,128)(2,1)} %gate.1, bf16[128,1792]{1,0:T(8,128)(2,1)} %up.1, bf16[128,1792]{1,0:T(8,128)(2,1)} %hid.1, s32[1,128]{1,0:T(1,128)} %bitcast.2, f32[64]{0:T(128)} %weight.1, f32[128,1792]{1,0:T(8,128)} %grad.1, ...), custom_call_target="tpu_custom_call" | custom-call | tf_op jit(solution)/shard_map/metagradient/pallas_call | solution.py:491
  85.4 2.7 %emit.1 = (f32[128,1792]{1,0:T(8,128)}, f32[1,64]{1,0:T(1,128)}) custom-call(bf16[1792,128]{1,0:T(8,128)(2,1)} %get-tuple-element.6.res, f32[8,128]{1,0:T(8,128)} %get-tuple-element.7.sums), custom_call_target="tpu_custom_call" | custom-call | tf_op jit(solution)/shard_map/emit/pallas_call | solution.py:532

commit v3 on v2

--- a/solution.py
+++ b/solution.py
@@ -21,6 +21,7 @@
 ROWS = 128
 COLS = 1792
 PART = 448
+HALF = 224
 TOK = 512
 TOKENS = 4096
 NSRC = 64
@@ -52,7 +53,7 @@
 IZ = RECV.take(1)
 N1 = RECV.take(3)
 CC = RECV.take(16)
-RX = RECV.take(12)
+RX = RECV.take(24)
 RZ = RECV.take(1)
 N2 = RECV.take(3)
 SEND = Slots()
@@ -73,6 +74,7 @@
     res, src_out,
     grad_v, mom_v, sec_v, adj_v, gate_v, up_v, hid_v,
     tok, tang, xb, acts, act, idb, norm1, norm2, proj, mixed, cb, cr, s0, s1, s2, r0, r1, r2, fin,
+    ids_v, weight_s, sums,
     ls, ss, rs,
 ):
     dp, tn = lax.axis_index("dp"), lax.axis_index("tensor")
@@ -154,17 +156,17 @@
         return total
 
     get_grad = fetch(grad, grad_v)
+    with mark("barrier"):
+        barrier = pltpu.get_barrier_semaphore()
+        for group in (groups[1], groups[0], groups[2]):
+            for to in group:
+                pl.semaphore_signal(barrier, inc=1, device_id=to, device_id_type=MESH)
     block = zl * 4 + y
     own_rows = pl.ds(pl.multiple_of(zh * ROWS, ROWS), ROWS)
     get_tok = [fetch(tokens.at[:, pl.ds(h * 256, 256)], tok.at[2 * block + h, own_rows, :]) for h in range(2)]
-    get_acts = [fetch(gate, gate_v), fetch(up, up_v), fetch(hid, hid_v)]
+    get_acts = [fetch(gate, gate_v), fetch(up, up_v), fetch(hid, hid_v), fetch(ids, ids_v), fetch(weight, weight_s)]
     get_rest = [fetch(mom, mom_v), fetch(sec, sec_v), fetch(adj, adj_v)]
-
-    with mark("barrier"):
-        barrier = pltpu.get_barrier_semaphore()
-        for group in groups:
-            for to in group:
-                pl.semaphore_signal(barrier, inc=1, device_id=to, device_id_type=MESH)
+    with mark("barrier_wait"):
         pl.semaphore_wait(barrier, sum(len(group) for group in groups))
 
     get_grad.wait()
@@ -200,10 +202,10 @@
 
     for copy in get_acts:
         copy.wait()
-    ids_row = ids[...]
+    ids_row = ids_v[...]
     weight_row = jnp.zeros((1, ROWS), F32)
     for k in range(NSRC):
-        weight_row = jnp.where(ids_row == k, weight[k], weight_row)
+        weight_row = jnp.where(ids_row == k, weight_s[k], weight_row)
     weight_row = weight_row / TOKENS
     idb[zh] = jnp.broadcast_to(ids_row.astype(F32), (8, ROWS))
 
@@ -232,9 +234,6 @@
         push(idb.at[zh], idb.at[zh], S_I, IZ, at_zh(zhs(d)))
     keep_act = [fetch(acts.at[k, part_rows(zh), :], act.at[k, zh]) for k in range(2)]
 
-    with mark("norm_a"):
-        spread(norm1, S_N1, N1, 1, collect(norm1, N1, 0))
-
     def forward_z(k):
         with mark(f"fz{k}"):
             z_at = zs(-k)
@@ -251,6 +250,8 @@
                 push(shard(z_at, y), shard(z_at, y), S_TZ, TZ + 4 + k, z_dev[-1])
             pass_y(2 * k, z_at)
 
+    with mark("norm_a"):
+        spread(norm1, S_N1, N1, 1, collect(norm1, N1, 0))
     forward_z(1)
     backward_z(1)
     with mark("norm_b"):
@@ -264,28 +265,37 @@
     for copy in get_rest:
         copy.wait()
 
-    def tangent(j, carry):
-        cols = pl.ds(pl.multiple_of(j * 128, 128), 128)
-        clipped = clip * grad_v[:, cols]
-        moment_new = BETA_ONE * mom_v[:, cols] + (1.0 - BETA_ONE) * clipped
-        second_new = BETA_TWO * sec_v[:, cols] + (1.0 - BETA_TWO) * clipped * clipped
-        root_v = jnp.sqrt(second_new)
-        inverse = 1.0 / (root_v + ADAM_EPSILON)
-        jacobian = -LEARN_RATE * (
-            (1.0 - BETA_ONE) * inverse - moment_new * (1.0 - BETA_TWO) * clipped * (inverse * inverse / root_v)
-        )
-        pulled = jacobian * adj_v[:, cols]
-        tang[cols, :] = (clip * pulled).T.astype(BF16)
-        return carry
-
-    with mark("tangent"):
-        lax.fori_loop(0, COLS // 128, tangent, 0)
-
-    keep = fetch(tang.at[part_rows(zh), :], xb.at[dp])
-    forward_z(3)
-    backward_z(3)
-    for d in (1, 3, 2):
-        push(tang.at[part_rows(zhs(d)), :], xb.at[dp], S_X, XZ + d, at_zh(zhs(d)))
+    def tangent(q):
+        first = lax.div(7 * q, 2)
+
+        def tile(j, carry):
+            cols = pl.ds(pl.multiple_of((first + j) * 128, 128), 128)
+            clipped = clip * grad_v[:, cols]
+            moment_new = BETA_ONE * mom_v[:, cols] + (1.0 - BETA_ONE) * clipped
+            second_new = BETA_TWO * sec_v[:, cols] + (1.0 - BETA_TWO) * clipped * clipped
+            root_v = jnp.sqrt(second_new)
+            inverse = 1.0 / (root_v + ADAM_EPSILON)
+            jacobian = -LEARN_RATE * (
+                (1.0 - BETA_ONE) * inverse - moment_new * (1.0 - BETA_TWO) * clipped * (inverse * inverse / root_v)
+            )
+            pulled = jacobian * adj_v[:, cols]
+            tang[q, pl.ds(pl.multiple_of(j * 128, 128), 128), :] = (clip * pulled).T.astype(BF16)
+            return carry
+
+        lax.fori_loop(0, 4, tile, 0)
+        return tang.at[q, pl.ds(pl.multiple_of(lax.rem(q, 2) * 64, 64), PART), :]
+
+    def x_first(d):
+        with mark(f"tangent{d}"):
+            push(tangent(zhs(d)), xb.at[dp], S_X, XZ + d, at_zh(zhs(d)))
+
+    x_first(1)
+    x_first(3)
+    x_first(2)
+    with mark("tangent0"):
+        keep = fetch(tangent(zh), xb.at[dp])
+    relay_y(1, zs(-1))
+    relay_y(2, zs(1))
 
     def x_block(x_at, d):
         return xb.at[zhs(-d) * 8 + x_at * 2 + c]
@@ -318,44 +328,51 @@
             push(there, there, S_X, XC, core)
 
     x_own(0)
-    relay_y(1, zs(-1))
-    relay_y(2, zs(1))
+    forward_z(3)
+    backward_z(3)
     x_sides(0)
-    relay_y(3, zs(-2))
-    forward_z(4)
     x_own(1)
     x_own(3)
+    share_acts(1)
+    relay_y(3, zs(-2))
+    relay_y(4, zs(2))
     x_relay(0)
-    relay_y(4, zs(2))
     x_own(2)
-    share_acts(1)
-    share_acts(0)
     x_sides(1)
     x_sides(3)
+    forward_z(4)
     relay_y(5, zs(-3))
+    relay_y(6, zs(3))
+    x_sides(2)
     x_relay(1)
     x_relay(3)
-    x_sides(2)
-    relay_y(6, zs(3))
+    relay_y(7, zs(-4))
+    share_acts(0)
     x_relay(2)
-    relay_y(7, zs(-4))
-
-    with mark("ylast"):
+
+    proj[...] = jnp.zeros_like(proj)
+
+    def first_product(y_at):
+        left = jnp.concatenate([xb[4 * k + i] for k in (y_at, y_at + 4) for i in range(4)], axis=1)
+        right = jnp.concatenate([tok[2 * k + i] for k in (y_at, y_at + 4) for i in range(2)], axis=1)
+        proj[...] += lax.dot_general(left, right, (((1,), (1,)), ((), ())), preferred_element_type=F32)
+
+    with mark("ynear"):
         arrived(tok.at[pl.ds(0, 4)], TY_AHEAD)
-        arrived(tok.at[pl.ds(0, 4)], TY_RELAY)
     with mark("xcore"):
         arrived(xb.at[pl.ds(0, 16)], XC)
 
-    proj[...] = jnp.zeros_like(proj)
-
-    def first_product(k, carry):
-        left = jnp.concatenate([xb[8 * k + i] for i in range(8)], axis=1)
-        right = jnp.concatenate([tok[4 * k + i] for i in range(4)], axis=1)
-        proj[...] += lax.dot_general(left, right, (((1,), (1,)), ((), ())), preferred_element_type=F32)
+    def near(k, carry):
+        first_product(lax.rem(y + 3 + k, 4))
         return carry
 
     with mark("product1"):
-        lax.fori_loop(0, 4, first_product, 0)
+        lax.fori_loop(0, 3, near, 0)
+    with mark("yfar"):
+        arrived(tok.at[pl.ds(0, 4)], TY_RELAY)
+
+    with mark("product1b"):
+        first_product(lax.rem(y + 2, 4))
 
     with mark("second_wait"):
         for copy in keep_act:
@@ -370,20 +387,20 @@
     def source_sums():
         arrived(act.at[0, pl.ds(0, 3)], AZ)
         arrived(idb.at[pl.ds(0, 3)], IZ)
-        sums = jnp.zeros((8, 128), F32)
+        total = jnp.zeros((8, 128), F32)
         source = lax.broadcasted_iota(jnp.int32, (128, ROWS), 0).astype(F32)
         for k in range(4):
             part = proj[:, pl.ds(k * ROWS, ROWS)]
             per_tok = jnp.sum(part * act[0, k].astype(F32), axis=0, keepdims=True)
             onehot = (source == idb[k, 0:1, :]).astype(F32)
-            sums = sums + lax.dot_general(
+            total = total + lax.dot_general(
                 jnp.broadcast_to(per_tok, (8, ROWS)),
                 onehot,
                 (((1,), (1,)), ((), ())),
                 precision=lax.Precision.HIGHEST,
                 preferred_element_type=F32,
             )
-        return sums
+        return total
 
     order = (2, 1, 3, 0)
     behind, ahead = 3 - 2 * c, 1 + 2 * c
@@ -395,71 +412,95 @@
         cb[x_at, zh_at, 1] = whole[:, 128:].astype(BF16)
         push(cb.at[x_at, zh_at, 1 - c], cr.at[x_at, zh_at], S_CC, CC + offset * 4 + j, core)
 
-    def both(offset, j):
+    def half(h):
+        return pl.ds(h * HALF, HALF)
+
+    def both(offset, j, h):
         x_at, zh_at = lax.rem(x + offset, 4), zhs(order[j])
-        arrived(cr.at[x_at, zh_at], CC + offset * 4 + j)
-        return cb[x_at, zh_at, c].astype(F32) + cr[x_at, zh_at].astype(F32)
-
-    def opposite(j):
-        with mark(f"opposite{j}"):
-            s0[j] = both(2, j).astype(BF16)
-            push(s0.at[j], r0.at[j], S_R, RX + j, x_dev[1])
-
-    def backward(j):
-        with mark(f"backward{j}"):
-            s2[j] = both(behind, j).astype(BF16)
-            push(s2.at[j], r2.at[j], S_R, RX + 8 + j, x_dev[-1])
-
-    def onward(j):
-        with mark(f"onward{j}"):
-            part = both(ahead, j)
-            arrived(r0.at[j], RX + j)
-            s1[j] = (part + r0[j].astype(F32)).astype(BF16)
-            push(s1.at[j], r1.at[j], S_R, RX + 4 + j, x_dev[1])
-
-    def finish(j):
-        with mark(f"finish{j}"):
-            part = both(0, j)
-            arrived(r2.at[j], RX + 8 + j)
-            part = part + r2[j].astype(F32)
-            arrived(r1.at[j], RX + 4 + j)
-            fin[j] = (part + r1[j].astype(F32)).astype(BF16)
+        if h == 0:
+            arrived(cr.at[x_at, zh_at], CC + offset * 4 + j)
+        return cb[x_at, zh_at, c, half(h)].astype(F32) + cr[x_at, zh_at, half(h)].astype(F32)
+
+    def opposite(j, h):
+        with mark(f"opposite{j}{h}"):
+            s0[j, half(h)] = both(2, j, h).astype(BF16)
+            push(s0.at[j, half(h)], r0.at[j, half(h)], S_R, RX + 2 * j + h, x_dev[1])
+
+    def backward(j, h):
+        with mark(f"backward{j}{h}"):
+            s2[j, half(h)] = both(behind, j, h).astype(BF16)
+            push(s2.at[j, half(h)], r2.at[j, half(h)], S_R, RX + 16 + 2 * j + h, x_dev[-1])
+
+    def onward(j, h):
+        with mark(f"onward{j}{h}"):
+            part = both(ahead, j, h)
+            arrived(r0.at[j, half(h)], RX + 2 * j + h)
+            s1[j, half(h)] = (part + r0[j, half(h)].astype(F32)).astype(BF16)
+            push(s1.at[j, half(h)], r1.at[j, half(h)], S_R, RX + 8 + 2 * j + h, x_dev[1])
+
+    def finish(j, h):
+        with mark(f"finish{j}{h}"):
+            part = both(0, j, h)
+            arrived(r2.at[j, half(h)], RX + 16 + 2 * j + h)
+            part = part + r2[j, half(h)].astype(F32)
+            arrived(r1.at[j, half(h)], RX + 8 + 2 * j + h)
+            fin[j, half(h)] = (part + r1[j, half(h)].astype(F32)).astype(BF16)
             d = order[j]
+            rows = pl.ds(pl.multiple_of(zh * PART + h * HALF, 32), HALF)
             if d:
-                push(fin.at[j], res.at[part_rows(zh), :], S_Z, RZ, at_zh(zhs(d)))
-            else:
+                push(fin.at[j, half(h)], res.at[rows, :], S_Z, RZ, at_zh(zhs(d)))
+            elif h:
                 fetch(fin.at[j], res.at[part_rows(zh), :])
 
     todo = (
-        (2, 0), (1, 0), (3, 0), (2, 1), (1, 1), (3, 1), (2, 2), (0, 0), (1, 2), (3, 2), (2, 3), (0, 1), (1, 3), (3, 3), (0, 2), (0, 3),
+        (2, 0), (1, 0), (3, 0), (2, 1), (1, 1), (3, 1), (2, 2), (1, 2), (3, 2), (0, 0), (2, 3), (1, 3), (3, 3), (0, 1), (0, 2), (0, 3),
     )
     then = {
-        4: [(opposite, 0)], 6: [(backward, 0)], 7: [(opposite, 1)], 9: [(backward, 1)], 10: [(opposite, 2)],
-        12: [(onward, 0)], 13: [(backward, 2)], 14: [(opposite, 3)], 15: [(onward, 1), (backward, 3)],
+        4: [(opposite, 0, 0), (opposite, 0, 1)],
+        6: [(backward, 0, 0), (backward, 0, 1)],
+        8: [(opposite, 1, 0)],
+        9: [(backward, 1, 0)],
+        11: [(onward, 0, 0), (onward, 0, 1)],
+        12: [(opposite, 2, 0), (backward, 2, 0)],
+        13: [(opposite, 1, 1), (backward, 1, 1)],
+        15: [(onward, 1, 0), (opposite, 2, 1), (backward, 2, 1)],
     }
     for i, (offset, j) in enumerate(todo):
         with mark(f"second{i}"):
             second_product(offset, j)
-        for step, at in then.get(i, ()):
-            step(at)
+        for step, at, h in then.get(i, ()):
+            step(at, h)
     with mark("n2_0"):
-        spread(norm2, S_N2, N2, 0, source_sums())
-    onward(2)
+        spread(norm2, S_N2, N2, 1, source_sums())
+    finish(0, 0)
+    finish(0, 1)
+    onward(2, 0)
+    onward(1, 1)
+    opposite(3, 0)
+    backward(3, 0)
+    finish(1, 0)
+    onward(2, 1)
+    opposite(3, 1)
+    backward(3, 1)
     with mark("n2_1"):
-        spread(norm2, S_N2, N2, 1, collect(norm2, N2, 0))
-    finish(0)
-    onward(3)
-    finish(1)
+        spread(norm2, S_N2, N2, 0, collect(norm2, N2, 1))
+    finish(2, 0)
+    finish(1, 1)
+    onward(3, 0)
+    finish(2, 1)
+    onward(3, 1)
     with mark("n2_2"):
-        spread(norm2, S_N2, N2, 2, collect(norm2, N2, 1))
-    finish(2)
-    finish(3)
+        spread(norm2, S_N2, N2, 2, collect(norm2, N2, 0))
+    finish(3, 0)
+    finish(3, 1)
     with mark("zlast"):
         arrived(cr.at[0, pl.ds(0, 3)], RZ)
     with mark("n2_3"):
-        src_out[...] = collect(norm2, N2, 2) / TOKENS
+        sums[...] = collect(norm2, N2, 2) / TOKENS
+        fetch(sums, src_out)
     with mark("drain"):
         local[-1].wait()
+        local[-2].wait()
         drained(tok.at[pl.ds(0, 7), pl.ds(0, 256)], S_TZ)
         drained(tok.at[pl.ds(0, 12)], S_TY)
         drained(xb.at[pl.ds(0, 31)], S_X)
@@ -487,18 +528,17 @@
 def body(tokens, gate_pre, up_act, hidden_cot, source_ids, data_weight, grad, moment_m, moment_v, val_adjoint):
     hbm = pl.BlockSpec(memory_space=pl.ANY)
     vmem = pl.BlockSpec(memory_space=pltpu.VMEM)
-    smem = pl.BlockSpec(memory_space=pltpu.SMEM)
     turned, sums = pl.pallas_call(
         kernel,
         name="metagradient",
         out_shape=(jax.ShapeDtypeStruct((COLS, ROWS), BF16), jax.ShapeDtypeStruct((8, 128), F32)),
-        in_specs=[hbm, hbm, hbm, hbm, vmem, smem, hbm, hbm, hbm, hbm],
-        out_specs=(hbm, vmem),
+        in_specs=[hbm] * 10,
+        out_specs=(hbm, hbm),
         scratch_shapes=[
             *[pltpu.VMEM((ROWS, COLS), F32)] * 4,
             *[pltpu.VMEM((ROWS, COLS), BF16)] * 3,
             pltpu.VMEM((16, TOK, 256), BF16),
-            pltpu.VMEM((COLS, ROWS), BF16),
+            pltpu.VMEM((4, 512, ROWS), BF16),
             pltpu.VMEM((32, PART, 128), BF16),
             pltpu.VMEM((2, COLS, ROWS), BF16),
             pltpu.VMEM((2, 4, PART, ROWS), BF16),
@@ -510,7 +550,10 @@
             pltpu.VMEM((4, 4, 2, PART, 128), BF16),
             pltpu.VMEM((4, 4, PART, 128), BF16),
             *[pltpu.VMEM((4, PART, 128), BF16)] * 7,
-            pltpu.SemaphoreType.DMA((14,)),
+            pltpu.VMEM((1, ROWS), jnp.int32),
+            pltpu.SMEM((NSRC,), F32),
+            pltpu.VMEM((8, 128), F32),
+            pltpu.SemaphoreType.DMA((16,)),
             pltpu.SemaphoreType.DMA((SEND.used,)),
             pltpu.SemaphoreType.DMA((RECV.used,)),
         ],

time: 88.3 us -> 78.8 us (0.89)
  Pallas kernels: 87.5 us -> 78.1 us
    pallas_call x1, Pallas kernels: 84.8 us -> 75.4 us  [body(): pl.pallas_call(kernel, name='metagradient', out_shape=(jax.ShapeDtypeStru...]
where the time goes in v3:
time: 78.8 us; the launch traced here: 78.7 us
  Pallas kernels  78.1 us (99%)
    pallas_call x1, Pallas kernels, body(): pl.pallas_call(kernel, name='metagradient', out_shape=(jax.ShapeDtypeStru...  75.4 us
    pallas_call x1, Pallas kernels, body(): pl.pallas_call(emit, name='emit', out_shape=(jax.ShapeDtypeStruct((ROWS,...  2.7 us

profile of v3, /device:TPU:1, one launch (start us, length us, event | category | flops | bytes accessed | tf_op | source)
XLA Modules:
  0.0 78.7 jit_solution(5698198537032663402)
XLA Ops:
  0.6 75.4 %metagradient.1 = (bf16[1792,128]{1,0:T(8,128)(2,1)}, f32[8,128]{1,0:T(8,128)}) custom-call(bf16[128,512]{1,0:T(8,128)(2,1)} %tokens.1, bf16[128,1792]{1,0:T(8,128)(2,1)} %gate.1, bf16[128,1792]{1,0:T(8,128)(2,1)} %up.1, bf16[128,1792]{1,0:T(8,128)(2,1)} %hid.1, s32[1,128]{1,0:T(1,128)} %bitcast.2, f32[64]{0:T(128)} %weight.1, f32[128,1792]{1,0:T(8,128)} %grad.1, ...), custom_call_target="tpu_custom_call" | custom-call | tf_op jit(solution)/shard_map/metagradient/pallas_call | solution.py:531
  76.0 2.7 %emit.1 = (f32[128,1792]{1,0:T(8,128)}, f32[1,64]{1,0:T(1,128)}) custom-call(bf16[1792,128]{1,0:T(8,128)(2,1)} %get-tuple-element.6.res, f32[8,128]{1,0:T(8,128)} %get-tuple-element.7.sums), custom_call_target="tpu_custom_call" | custom-call | tf_op jit(solution)/shard_map/emit/pallas_call | solution.py:575

commit v4 on v3

--- a/solution.py
+++ b/solution.py
@@ -74,7 +74,7 @@
     res, src_out,
     grad_v, mom_v, sec_v, adj_v, gate_v, up_v, hid_v,
     tok, tang, xb, acts, act, idb, norm1, norm2, proj, mixed, cb, cr, s0, s1, s2, r0, r1, r2, fin,
-    ids_v, weight_s, sums,
+    ids_v, weight_s, sums, onehot,
     ls, ss, rs,
 ):
     dp, tn = lax.axis_index("dp"), lax.axis_index("tensor")
@@ -207,6 +207,7 @@
     for k in range(NSRC):
         weight_row = jnp.where(ids_row == k, weight_s[k], weight_row)
     weight_row = weight_row / TOKENS
+    weight_col = jnp.broadcast_to(weight_row, (ROWS, ROWS)).T
     idb[zh] = jnp.broadcast_to(ids_row.astype(F32), (8, ROWS))
 
     def activation(j, carry):
@@ -216,8 +217,8 @@
         coupling = up_v[:, cols].astype(F32) * hid_v[:, cols].astype(F32)
         first = coupling * sigma * (1.0 + pre * (1.0 - sigma))
         second = coupling * sigma * (1.0 - sigma) * (2.0 + pre * (1.0 - 2.0 * sigma))
-        acts[0, cols, :] = first.T.astype(BF16)
-        acts[1, cols, :] = (second.T * weight_row).astype(BF16)
+        acts[0, cols, :] = first.astype(BF16).T
+        acts[1, cols, :] = (second * weight_col).astype(BF16).T
         return carry
 
     with mark("activation"):
@@ -279,7 +280,7 @@
                 (1.0 - BETA_ONE) * inverse - moment_new * (1.0 - BETA_TWO) * clipped * (inverse * inverse / root_v)
             )
             pulled = jacobian * adj_v[:, cols]
-            tang[q, pl.ds(pl.multiple_of(j * 128, 128), 128), :] = (clip * pulled).T.astype(BF16)
+            tang[q, pl.ds(pl.multiple_of(j * 128, 128), 128), :] = (clip * pulled).astype(BF16).T
             return carry
 
         lax.fori_loop(0, 4, tile, 0)
@@ -348,31 +349,28 @@
     x_relay(3)
     relay_y(7, zs(-4))
     share_acts(0)
+    arrived(idb.at[pl.ds(0, 3)], IZ)
+    source = lax.broadcasted_iota(jnp.int32, (128, ROWS), 0).astype(F32)
+    for k in range(4):
+        onehot[:, k * ROWS : (k + 1) * ROWS] = (source == idb[k, 0:1, :]).astype(F32)
     x_relay(2)
 
-    proj[...] = jnp.zeros_like(proj)
-
-    def first_product(y_at):
-        left = jnp.concatenate([xb[4 * k + i] for k in (y_at, y_at + 4) for i in range(4)], axis=1)
-        right = jnp.concatenate([tok[2 * k + i] for k in (y_at, y_at + 4) for i in range(2)], axis=1)
-        proj[...] += lax.dot_general(left, right, (((1,), (1,)), ((), ())), preferred_element_type=F32)
+    def first_product(places):
+        blocks = [k for y_at in places for k in (y_at, y_at + 4)]
+        left = jnp.concatenate([xb[4 * k + i] for k in blocks for i in range(4)], axis=1)
+        right = jnp.concatenate([tok[2 * k + i] for k in blocks for i in range(2)], axis=1)
+        return lax.dot_general(left, right, (((1,), (1,)), ((), ())), preferred_element_type=F32)
 
     with mark("ynear"):
         arrived(tok.at[pl.ds(0, 4)], TY_AHEAD)
     with mark("xcore"):
         arrived(xb.at[pl.ds(0, 16)], XC)
-
-    def near(k, carry):
-        first_product(lax.rem(y + 3 + k, 4))
-        return carry
-
     with mark("product1"):
-        lax.fori_loop(0, 3, near, 0)
+        proj[...] = first_product([y, ys(-1), ys(1)])
     with mark("yfar"):
         arrived(tok.at[pl.ds(0, 4)], TY_RELAY)
-
     with mark("product1b"):
-        first_product(lax.rem(y + 2, 4))
+        proj[...] += first_product([ys(2)])
 
     with mark("second_wait"):
         for copy in keep_act:
@@ -386,24 +384,30 @@
 
     def source_sums():
         arrived(act.at[0, pl.ds(0, 3)], AZ)
-        arrived(idb.at[pl.ds(0, 3)], IZ)
-        total = jnp.zeros((8, 128), F32)
-        source = lax.broadcasted_iota(jnp.int32, (128, ROWS), 0).astype(F32)
-        for k in range(4):
-            part = proj[:, pl.ds(k * ROWS, ROWS)]
-            per_tok = jnp.sum(part * act[0, k].astype(F32), axis=0, keepdims=True)
-            onehot = (source == idb[k, 0:1, :]).astype(F32)
-            total = total + lax.dot_general(
-                jnp.broadcast_to(per_tok, (8, ROWS)),
-                onehot,
-                (((1,), (1,)), ((), ())),
-                precision=lax.Precision.HIGHEST,
-                preferred_element_type=F32,
-            )
-        return total
+        per_tok = [
+            jnp.sum(proj[:, pl.ds(k * ROWS, ROWS)] * act[0, k].astype(F32), axis=0, keepdims=True) for k in range(4)
+        ]
+        return lax.dot_general(
+            jnp.broadcast_to(jnp.concatenate(per_tok, axis=1), (8, TOK)),
+            onehot[...],
+            (((1,), (1,)), ((), ())),
+            precision=lax.Precision.HIGHEST,
+            preferred_element_type=F32,
+        )
 
     order = (2, 1, 3, 0)
     behind, ahead = 3 - 2 * c, 1 + 2 * c
+
+    def pair_product(j):
+        zh_at = zhs(order[j])
+        at = [lax.rem(x + offset, 4) for offset in (1, 3)]
+        right = jnp.concatenate([tok[zh_at * 4 + x_at] for x_at in at], axis=1)
+        whole = jnp.dot(mixed[...], right, preferred_element_type=F32)
+        for k, x_at in enumerate(at):
+            for half_at in range(2):
+                cols = slice(256 * k + 128 * half_at, 256 * k + 128 * half_at + 128)
+                cb[x_at, zh_at, half_at] = whole[:, cols].astype(BF16)
+            push(cb.at[x_at, zh_at, 1 - c], cr.at[x_at, zh_at], S_CC, CC + (1 + 2 * k) * 4 + j, core)
 
     def second_product(offset, j):
         x_at, zh_at = lax.rem(x + offset, 4), zhs(order[j])
@@ -467,7 +471,10 @@
     }
     for i, (offset, j) in enumerate(todo):
         with mark(f"second{i}"):
-            second_product(offset, j)
+            if offset == 1:
+                pair_product(j)
+            elif offset != 3:
+                second_product(offset, j)
         for step, at, h in then.get(i, ()):
             step(at, h)
     with mark("n2_0"):
@@ -479,25 +486,25 @@
     opposite(3, 0)
     backward(3, 0)
     finish(1, 0)
+    with mark("n2_1"):
+        spread(norm2, S_N2, N2, 0, collect(norm2, N2, 1))
     onward(2, 1)
     opposite(3, 1)
     backward(3, 1)
-    with mark("n2_1"):
-        spread(norm2, S_N2, N2, 0, collect(norm2, N2, 1))
     finish(2, 0)
     finish(1, 1)
+    with mark("n2_2"):
+        spread(norm2, S_N2, N2, 2, collect(norm2, N2, 0))
     onward(3, 0)
     finish(2, 1)
     onward(3, 1)
-    with mark("n2_2"):
-        spread(norm2, S_N2, N2, 2, collect(norm2, N2, 0))
     finish(3, 0)
     finish(3, 1)
-    with mark("zlast"):
-        arrived(cr.at[0, pl.ds(0, 3)], RZ)
     with mark("n2_3"):
         sums[...] = collect(norm2, N2, 2) / TOKENS
         fetch(sums, src_out)
+    with mark("zlast"):
+        arrived(cr.at[0, pl.ds(0, 3)], RZ)
     with mark("drain"):
         local[-1].wait()
         local[-2].wait()
@@ -518,10 +525,10 @@
 def emit(res, sums, out, src):
     def turn(j, carry):
         cols = pl.ds(pl.multiple_of(j * 128, 128), 128)
-        out[:, cols] = res[cols, :].astype(F32).T
+        out[:, cols] = res[cols, :].T.astype(F32)
         return carry
 
-    lax.fori_loop(0, COLS // 128, turn, 0, unroll=2)
+    lax.fori_loop(0, COLS // 128, turn, 0, unroll=14)
     src[...] = sums[0:1, :NSRC]
 
 
@@ -553,6 +560,7 @@
             pltpu.VMEM((1, ROWS), jnp.int32),
             pltpu.SMEM((NSRC,), F32),
             pltpu.VMEM((8, 128), F32),
+            pltpu.VMEM((128, TOK), F32),
             pltpu.SemaphoreType.DMA((16,)),
             pltpu.SemaphoreType.DMA((SEND.used,)),
             pltpu.SemaphoreType.DMA((RECV.used,)),

time: 78.8 us -> 77.4 us (0.982)
  Pallas kernels: 78.1 us -> 76.6 us
    pallas_call x1, Pallas kernels: 75.4 us -> 74.5 us  [body(): pl.pallas_call(kernel, name='metagradient', out_shape=(jax.ShapeDtypeStru...]
where the time goes in v4:
time: 77.4 us; the launch traced here: 77.3 us
  Pallas kernels  76.6 us (99%)
    pallas_call x1, Pallas kernels, body(): pl.pallas_call(kernel, name='metagradient', out_shape=(jax.ShapeDtypeStru...  74.5 us
    pallas_call x1, Pallas kernels, body(): pl.pallas_call(emit, name='emit', out_shape=(jax.ShapeDtypeStruct((ROWS,...  2.12 us

profile of v4, /device:TPU:1, one launch (start us, length us, event | category | flops | bytes accessed | tf_op | source)
XLA Modules:
  0.0 77.3 jit_solution(2889275719295321134)
XLA Ops:
  0.6 74.5 %metagradient.1 = (bf16[1792,128]{1,0:T(8,128)(2,1)}, f32[8,128]{1,0:T(8,128)}) custom-call(bf16[128,512]{1,0:T(8,128)(2,1)} %tokens.1, bf16[128,1792]{1,0:T(8,128)(2,1)} %gate.1, bf16[128,1792]{1,0:T(8,128)(2,1)} %up.1, bf16[128,1792]{1,0:T(8,128)(2,1)} %hid.1, s32[1,128]{1,0:T(1,128)} %bitcast.2, f32[64]{0:T(128)} %weight.1, f32[128,1792]{1,0:T(8,128)} %grad.1, ...), custom_call_target="tpu_custom_call" | custom-call | tf_op jit(solution)/shard_map/metagradient/pallas_call | solution.py:538
  75.1 2.1 %emit.1 = (f32[128,1792]{1,0:T(8,128)}, f32[1,64]{1,0:T(1,128)}) custom-call(bf16[1792,128]{1,0:T(8,128)(2,1)} %get-tuple-element.6.res, f32[8,128]{1,0:T(8,128)} %get-tuple-element.7.sums), custom_call_target="tpu_custom_call" | custom-call | tf_op jit(solution)/shard_map/emit/pallas_call | solution.py:583

commit v5 on v4

--- a/solution.py
+++ b/solution.py
@@ -227,8 +227,8 @@
     def part_rows(q):
         return pl.ds(pl.multiple_of(q * PART, 64), PART)
 
-    def share_acts(which):
-        for d in (2, 1, 3):
+    def share_acts(which, partners=(1, 3, 2)):
+        for d in partners:
             push(acts.at[which, part_rows(zhs(d)), :], act.at[which, zh], S_A + which, AZ + which, at_zh(zhs(d)))
 
     for d in (1, 2, 3):
@@ -334,11 +334,12 @@
     x_sides(0)
     x_own(1)
     x_own(3)
-    share_acts(1)
+    share_acts(1, (1, 3))
     relay_y(3, zs(-2))
     relay_y(4, zs(2))
     x_relay(0)
     x_own(2)
+    share_acts(1, (2,))
     x_sides(1)
     x_sides(3)
     forward_z(4)
@@ -523,12 +524,8 @@
 
 
 def emit(res, sums, out, src):
-    def turn(j, carry):
-        cols = pl.ds(pl.multiple_of(j * 128, 128), 128)
-        out[:, cols] = res[cols, :].T.astype(F32)
-        return carry
-
-    lax.fori_loop(0, COLS // 128, turn, 0, unroll=14)
+    for j in range(7):
+        out[:, j * 128 : (j + 1) * 128] = res[j * 128 : (j + 1) * 128, :].T.astype(F32)
     src[...] = sums[0:1, :NSRC]
 
 
@@ -584,8 +581,9 @@
         emit,
         name="emit",
         out_shape=(jax.ShapeDtypeStruct((ROWS, COLS), F32), jax.ShapeDtypeStruct((1, NSRC), F32)),
-        in_specs=[vmem, vmem],
-        out_specs=(vmem, vmem),
+        grid=(2,),
+        in_specs=[pl.BlockSpec((COLS // 2, ROWS), lambda i: (i, 0)), pl.BlockSpec((8, 128), lambda i: (0, 0))],
+        out_specs=(pl.BlockSpec((ROWS, COLS // 2), lambda i: (0, i)), pl.BlockSpec((1, NSRC), lambda i: (0, 0))),
         compiler_params=pltpu.CompilerParams(vmem_limit_bytes=60 * 2**20),
     )(turned, sums)
     return curvature, source_grad.reshape(NSRC)

time: 77.4 us -> 78.6 us (1.016)
  the two profiles are of different devices: /device:TPU:1 before, /device:TPU:8 now
where the time goes in v5:
time: 78.6 us; the launch traced here: 78.5 us
  Pallas kernels  77.9 us (99%)
    pallas_call x1, Pallas kernels, body(): pl.pallas_call(kernel, name='metagradient', out_shape=(jax.ShapeDtypeStru...  75.9 us
    pallas_call x1, Pallas kernels, body(): pl.pallas_call(emit, name='emit', out_shape=(jax.ShapeDtypeStruct((ROWS,...  2 us

profile of v5, /device:TPU:8, one launch (start us, length us, event | category | flops | bytes accessed | tf_op | source)
XLA Modules:
  0.0 78.5 jit_solution(460442212019307320)
XLA Ops:
  0.6 75.9 %metagradient.1 = (bf16[1792,128]{1,0:T(8,128)(2,1)}, f32[8,128]{1,0:T(8,128)}) custom-call(bf16[128,512]{1,0:T(8,128)(2,1)} %tokens.1, bf16[128,1792]{1,0:T(8,128)(2,1)} %gate.1, bf16[128,1792]{1,0:T(8,128)(2,1)} %up.1, bf16[128,1792]{1,0:T(8,128)(2,1)} %hid.1, s32[1,128]{1,0:T(1,128)} %bitcast.2, f32[64]{0:T(128)} %weight.1, f32[128,1792]{1,0:T(8,128)} %grad.1, ...), custom_call_target="tpu_custom_call" | custom-call | tf_op jit(solution)/shard_map/metagradient/pallas_call | solution.py:535
  76.5 2.0 %emit.1 = (f32[128,1792]{1,0:T(8,128)}, f32[1,64]{1,0:T(1,128)}) custom-call(bf16[1792,128]{1,0:T(8,128)(2,1)} %get-tuple-element.6.res, f32[8,128]{1,0:T(8,128)} %get-tuple-element.7.sums), custom_call_target="tpu_custom_call" | custom-call | tf_op jit(solution)/shard_map/emit/pallas_call | solution.py:580
